TPU v7x, 768 devices: a whole 4x8x12 slice. The times are simulated.
768 devices in a mesh: aux: 48 (over x, z), orb: 16 (over y, core).
Axes of the slice: x: 4, y: 8, z: 12, core: 2. Of those that a mesh axis runs over, the one named last changes fastest.
Arguments:
- three_centre: bfloat16 [192, 2048, 2048], P('aux', 'orb'), may hold values from -0.125 to 0.125
- screening: int32 [192, 16, 16], P('aux', 'orb'), may hold values 0 or 1
- coefficients: bfloat16 [2048, 768], replicated, may hold values from -0.015625 to 0.015625
- occ_pattern: int32 [16, 48], replicated, may hold values 0 or 1
Outputs:
- exchange_matrix: float32 [2048, 2048], P('orb')
All inputs are finite; a program needn't handle non-finite values. No bound on the sum of `screening` on one device may be relied on, other than what follows from the above.
Results may differ from a plain program's by a relative error of at most 0.0015.
Values may be sent and summed in bfloat16 or wider, within the bound.
A program may use at most 64 MiB of HBM per device.

v0:
```python
import jax
import jax.numpy as jnp
from jax import lax
from jax.sharding import PartitionSpec as P


def on_device(three_centre, screening, coefficients, occ_pattern):
    aux_here, blk_rows, orbitals = three_centre.shape
    nblocks = screening.shape[2]
    block_width = orbitals // nblocks
    nslices = occ_pattern.shape[1]
    occupied = coefficients.shape[1]
    occ_mask = occ_pattern.astype(jnp.bfloat16)
    masked_c = (
        coefficients.reshape(nblocks, block_width, nslices, occupied // nslices)
        * occ_mask[:, None, :, None]
    ).reshape(orbitals, occupied)
    screen = screening[:, 0, :].astype(jnp.bfloat16)
    masked = (
        three_centre.reshape(aux_here, blk_rows, nblocks, block_width) * screen[:, None, :, None]
    ).reshape(aux_here, blk_rows, orbitals)
    halves = jnp.einsum("pmv,vi->ipm", masked, masked_c, preferred_element_type=jnp.float32).astype(
        jnp.bfloat16
    )
    partial_value = lax.dot_general(
        halves,
        lax.all_gather(halves, "orb", axis=2, tiled=True),
        (((0, 1), (0, 1)), ((), ())),
        preferred_element_type=jnp.float32,
    )
    result = lax.psum(partial_value, "aux")
    return result


def solution(mesh):
    return jax.shard_map(
        on_device,
        mesh=mesh,
        in_specs=(P("aux", "orb", None), P("aux", "orb", None), P(), P()),
        out_specs=P("orb", None),
        check_vma=False,
    )
```

profile of v0, /device:TPU:1, one launch (start us, length us, event | category | flops | bytes accessed | tf_op | source)
XLA Modules:
  0.0 346.3 jit_solution(15440146581576398565)
XLA Ops:
  6.5 0.0 all-gather.2.cloned.1.call-start
  6.5 0.7 convert_element_type.17
  7.2 0.7 convert_element_type.16
  7.9 0.1 copy.7
  8.0 0.1 broadcast_bitcast_fusion
  8.1 3.2 copy.8
  11.3 0.0 copy-start
  11.3 0.5 mul.24
  11.8 1.1 copy-done
  12.9 2.8 fusion.5
  15.7 0.0 all-gather.2.cloned.1.call-update
  15.7 0.0 all-reduce.2.cloned.1.call-start
  15.7 96.4 %all-gather.2.cloned.1.call-done = bf16[768,4,2048]{2,0,1:T(8,128)(2,1)} async-done(((bf16[768,4,128]{2,0,1:T(8,128)(2,1)}), bf16[768,4,2048]{2,0,1:T(8,128)(2,1)}) %all-gather.2.cloned.1.call-update) | async-done | bytes 12582928 | tf_op jit(solution)/shard_map/all_gather | solution.py:27
  112.1 7.6 %convolution_bitcast_fusion = f32[128,2048]{1,0:T(8,128)} fusion(bf16[768,4,128]{2,0,1:T(8,128)(2,1)} %fusion.5, bf16[768,4,2048]{2,0,1:T(8,128)(2,1)} %all-gather.2.cloned.1.call-done), kind=kOutput, calls=%fused_computation.4 | convolution fusion | flops 1610612736 | bytes 14417920 | tf_op jit(solution)/shard_map/dot_general | solution.py:25
  119.7 0.0 all-reduce.2.cloned.1.call-update
  119.8 217.4 %all-reduce.2.cloned.1.call-done = f32[128,2048]{1,0:T(8,128)} async-done(((f32[128,2048]{1,0:T(8,128)}), f32[128,2048]{1,0:T(8,128)}) %all-reduce.2.cloned.1.call-update) | async-done | bytes 1048592 | tf_op jit(solution)/shard_map/psum | solution.py:31
  337.2 2.3 copy.25
  (2 shorter events, 0.0 us)
Async XLA Ops:
  6.5 105.6 %all-gather.2.cloned.1.call-start = ((), (), s32[]{:S(2)}) async-start(), calls=%async_computation | async-start | bytes 13369344 | tf_op jit(solution)/shard_map/all_gather | solution.py:27
  11.3 1.6 copy-start
  15.7 321.5 %all-reduce.2.cloned.1.call-start = ((), (), s32[]{:S(2)}) async-start(), calls=%async_computation.1 | async-start | bytes 2097152 | tf_op jit(solution)/shard_map/psum | solution.py:31
Sparse Core Ops, SparseCore 0:
  15.8 96.2 all-gather.1
  119.9 217.2 all-reduce.1
where the time goes:
time: 353 us; the launch traced here: 346 us
  waiting for transfers between devices  314 us (89%)
  between operations  13.4 us (4%)
  matrix products  10.4 us (3%)
  local copies, waits for them, and re-layouts  7.25 us (2%)
    psum x1, waiting for transfers between devices, on_device(): result = lax.psum(partial_value, 'aux')  217 us
    all_gather x1, waiting for transfers between devices, on_device(): lax.all_gather(halves, 'orb', axis=2, tiled=True)  96.4 us
    dot_general x1, matrix products, on_device(): lax.dot_general(halves, lax.all_gather(halves, 'orb', axis=2, tiled=True)...  7.63 us
  transfers between devices with their start and end apart: 2, of which 2 were waited for; matrix products, arithmetic and copies ran while one was open for 0% of the time, Pallas kernels for 0%

commit v1 on v0

v1 whole, which is shorter than its diff:
```python
import jax
import jax.numpy as jnp
from jax import lax
from jax.experimental import pallas as pl
from jax.experimental.pallas import tpu as pltpu
from jax.sharding import PartitionSpec as P

MESH = pl.DeviceIdType.MESH
X, Y, Z = 4, 8, 12
BLK = 128
NT = (((1,), (1,)), ((), ()))


def kernel(t_hbm, scr_ref, c_hbm, occ_ref, out_ref,
           tv, cv, h, ring, blk, swp, xr, xs, zr, zt, ze, zf, full,
           load_sem, part_s, part_r, ring_s, ring_r, swp_s, swp_r,
           xs_s, xs_r, zs_s, zs_r, e_s, e_r, zg_s, zg_r, xg_s, xg_r):
    aux = lax.axis_index("aux")
    orb = lax.axis_index("orb")
    x, z = aux // Z, aux % Z
    y, core = orb // 2, orb % 2
    other = 1 - core
    high = y // 4
    sg, kk, hh = z // 4, (z // 2) % 2, z % 2
    nocc = cv.shape[1]

    def dev(xx, zz, yy, cc):
        return (xx * Z + zz, yy * 2 + cc)

    def remote(src, dst, s_sem, r_sem, where):
        return pltpu.make_async_remote_copy(
            src_ref=src, dst_ref=dst, send_sem=s_sem, recv_sem=r_sem,
            device_id=where, device_id_type=MESH)

    partner = dev(x, z, y, other)
    nexts = (dev(x, z, (y + Y - 1) % Y, core), dev(x, z, (y + 1) % Y, core))

    def mirror(g):
        s = g + 1
        dy = ((sg - 1) * (sg - 2) // 2) * s + sg * (2 - sg) * (Y - s) + (sg * (sg - 1) // 2) * 4
        flip = ((sg - 1) * (sg - 2) // 2) + (sg * (sg - 1) // 2) * 2
        return dev(x, 4 * flip + 2 * core + hh, (y + dy) % Y, kk)

    def x_peer(d):
        return dev((x + d) % X, z, y, core)

    def z_peer(d):
        return dev(x, (z + d) % Z, y, core)

    def load_t(p):
        return pltpu.make_async_copy(t_hbm.at[p], tv.at[p], load_sem.at[p])

    crows = cv.shape[0] // 4

    def load_c(q):
        rows = pl.ds(q * crows, crows)
        return pltpu.make_async_copy(c_hbm.at[rows], cv.at[rows], load_sem.at[4 + q])

    for q in range(4):
        load_c(q).start()
    for p in range(4):
        load_t(p).start()

    barrier = pltpu.get_barrier_semaphore()

    def signal(where):
        pl.semaphore_signal(barrier, inc=1, device_id=where, device_id_type=MESH)

    signal(partner)
    signal(nexts[0])
    signal(nexts[1])
    for d in range(1, X):
        signal(x_peer(d))

    @pl.loop(1, Z)
    def _(d):
        signal(z_peer(d))

    signal(mirror(2))

    @pl.when(z < 8)
    def _():
        signal(mirror(0))
        signal(mirror(1))

    occ = occ_ref[...].astype(jnp.float32).astype(jnp.bfloat16)
    nslices = occ.shape[1]
    spread = (lax.broadcasted_iota(jnp.int32, (nslices, nocc), 1) // (nocc // nslices)
              == lax.broadcasted_iota(jnp.int32, (nslices, nocc), 0)).astype(jnp.float32).astype(jnp.bfloat16)
    occ_mask = jnp.dot(occ, spread, preferred_element_type=jnp.float32).astype(jnp.bfloat16)
    screen = scr_ref[...].reshape(4, 16).astype(jnp.float32).astype(jnp.bfloat16)
    widen = (lax.broadcasted_iota(jnp.int32, (16, 2048), 1) // BLK
             == lax.broadcasted_iota(jnp.int32, (16, 2048), 0)).astype(jnp.float32).astype(jnp.bfloat16)
    scr_mask = jnp.dot(screen, widen, preferred_element_type=jnp.float32).astype(jnp.bfloat16)

    for q in range(4):
        load_c(q).wait()
        for nb in range(4 * q, 4 * q + 4):
            rows = slice(nb * BLK, (nb + 1) * BLK)
            cv[rows, :] = cv[rows, :] * occ_mask[nb:nb + 1, :]

    for p in range(4):
        load_t(p).wait()
        tv[p] = tv[p] * scr_mask[p:p + 1, :]

    pl.semaphore_wait(barrier, 20 - 2 * (z // 8))

    def hop(d, slot):
        if slot < 2:
            src = h.at[core, slot, d]
        elif slot < 6:
            src = ring.at[d, slot - 2]
        else:
            target = (y + Y - 1) % Y if d == 0 else (y + 1) % Y
            src = ring.at[d, 4 + target // 4]
        return remote(src, ring.at[d, slot], ring_s.at[d, slot], ring_r.at[d, slot], nexts[d])

    def to_partner(t, d):
        return remote(h.at[core, t, d], h.at[core, t, d], part_s.at[t, d], part_r.at[t, d], partner)

    for t in range(2):
        lhs = tv[2 * t:2 * t + 2].reshape(2 * BLK, tv.shape[2])
        for n in range(nocc // 256):
            cols = slice(n * 256, (n + 1) * 256)
            r = jnp.dot(lhs, cv[:, cols], preferred_element_type=jnp.float32).astype(jnp.bfloat16)
            h[core, t, 0, :, cols] = r[:BLK]
            h[core, t, 1, :, cols] = r[BLK:]
        for d in range(2):
            hop(d, t).start()
        for d in range(2):
            to_partner(t, d).start()

    def dot_nt(a, b):
        return lax.dot_general(a, b, NT, preferred_element_type=jnp.float32)

    for t in range(2):
        for d in range(2):
            to_partner(t, d).wait_recv()
    for who, put in ((core, "own"), (other, "swap")):
        total = None
        for t in range(2):
            for d in range(2):
                v = dot_nt(h[who, t, d], h[core, t, d])
                total = v if total is None else total + v
        if put == "own":
            blk[0, core, 2] = total
        else:
            swp[0, 2] = total
    blk[1, core, 2] = jnp.zeros((BLK, BLK), jnp.float32)
    swp[1, 2] = jnp.zeros((BLK, BLK), jnp.float32)

    def pair(who, t, d, slot, rows_own):
        a, b = h[who, t, d], ring[d, slot]
        return dot_nt(a, b) if rows_own else dot_nt(b, a)

    def ring_step(s, t):
        slot = 2 * (s - 1) + t
        for d in range(2):
            hop(d, slot).wait_recv()
            if slot < 4:
                hop(d, slot + 2).start()
            elif slot == 5:
                hop(d, 6).start()
        for d in range(2):
            own = pair(core, t, d, slot, d == 0)
            away = pair(other, t, d, slot, d == 0)
            if t == 0:
                blk[s - 1, core, d] = own
                swp[s - 1, d] = away
            else:
                blk[s - 1, core, d] += own
                swp[s - 1, d] += away

    def antipode():
        for d in range(2):
            hop(d, 6).wait_recv()

        for side in range(2):
            @pl.when(high == side)
            def _():
                blk[2, core, 2] = pair(core, side, 0, 6, side == 0) + pair(core, side, 1, 6, side == 0)
                swp[2, 2] = pair(other, side, 0, 6, side == 0) + pair(other, side, 1, 6, side == 0)

    def swap(g):
        return remote(swp.at[g], blk.at[g, core], swp_s.at[g], swp_r.at[g], partner)

    def wait_bytes(ref, sem):
        pltpu.make_async_copy(ref, ref, sem).wait()

    def swap_start(g):
        swap(g).start()

    def xrs_start(g):
        swap(g).wait_recv()
        for d in range(1, X):
            xx = (x + d) % X
            remote(blk.at[g, :, :, pl.ds(pl.multiple_of(xx * 32, 32), 32), :], xr.at[g, d - 1],
                   xs_s.at[g], xs_r.at[g], x_peer(d)).start()

    def zrs_start(g):
        wait_bytes(xr.at[g], xs_r.at[g])
        mine = blk[g, :, :, pl.ds(pl.multiple_of(x * 32, 32), 32), :]
        xs[g] = (mine + xr[g, 0]) + (xr[g, 1] + xr[g, 2])

        @pl.loop(1, Z)
        def _(d):
            zz = (z + d) % Z
            remote(xs.at[g, (zz // 2) % 2, zz // 4, pl.ds(pl.multiple_of((zz % 2) * 16, 16), 16), :],
                   zr.at[g, d - 1], zs_s.at[g], zs_r.at[g], z_peer(d)).start()

    def exchange(g):
        return remote(zt.at[g], ze.at[g], e_s.at[g], e_r.at[g], mirror(g))

    def when_mirrored(g, fn):
        if g == 2:
            fn()
        else:
            pl.when(z < 8)(fn)

    def ex_start(g):
        wait_bytes(zr.at[g], zs_r.at[g])
        total = xs[g, kk, sg, pl.ds(pl.multiple_of(hh * 16, 16), 16), :]
        for d in range(Z - 1):
            total = total + zr[g, d]
        zt[g] = total
        when_mirrored(g, lambda: exchange(g).start())

    def my_tile(g):
        return full.at[g, kk, sg, pl.ds(pl.multiple_of(x * 32 + hh * 16, 16), 16), :]

    def zag_start(g):
        def add():
            exchange(g).wait_recv()
            zf[g] = zt[g] + ze[g]

        when_mirrored(g, add)
        if g != 2:
            @pl.when(z >= 8)
            def _():
                zf[g] = zt[g]
        my_tile(g)[...] = zf[g]

        @pl.loop(1, Z)
        def _(d):
            remote(zf.at[g], my_tile(g), zg_s.at[g], zg_r.at[g], z_peer(d)).start()

    def x_slab(g):
        return full.at[g, :, :, pl.ds(pl.multiple_of(x * 32, 32), 32), :]

    def xag_start(g):
        wait_bytes(zr.at[g], zg_r.at[g])
        for d in range(1, X):
            remote(x_slab(g), x_slab(g), xg_s.at[g], xg_r.at[g], x_peer(d)).start()

    def put(d, k, value):
        out_ref[:, pl.ds(pl.multiple_of((2 * d + k) * BLK, BLK), BLK)] = value

    def finish(g):
        wait_bytes(xr.at[g], xg_r.at[g])
        s = g + 1
        for k in range(2):
            put((y + s) % Y, k, full[g, k, 0])
            put((y + Y - s) % Y, k, full[g, k, 1].T)
            if g == 0:
                put(y, k, full[g, k, 2])
        if g == 2:
            for side in range(2):
                @pl.when(high == side)
                def _():
                    for k in range(2):
                        v = full[g, k, 2]
                        put((y + 4) % Y, k, v if side == 0 else v.T)

    ring_step(1, 0)
    ring_step(1, 1)
    swap_start(0)
    ring_step(2, 0)
    xrs_start(0)
    ring_step(2, 1)
    swap_start(1)
    zrs_start(0)
    ring_step(3, 0)
    ex_start(0)
    xrs_start(1)
    ring_step(3, 1)
    zag_start(0)
    zrs_start(1)
    antipode()
    swap_start(2)
    xag_start(0)
    xrs_start(2)
    ex_start(1)
    zag_start(1)
    zrs_start(2)
    finish(0)
    xag_start(1)
    ex_start(2)
    zag_start(2)
    finish(1)
    xag_start(2)
    finish(2)

    for t in range(2):
        for d in range(2):
            to_partner(t, d).wait_send()
    for d in range(2):
        for slot in range(7):
            hop(d, slot).wait_send()
    for g in range(3):
        swap(g).wait_send()
        wait_bytes(xr.at[g], xs_s.at[g])
        wait_bytes(zr.at[g], zs_s.at[g])
        when_mirrored(g, lambda: exchange(g).wait_send())
        wait_bytes(zr.at[g], zg_s.at[g])
        wait_bytes(xr.at[g], xg_s.at[g])


def on_device(three_centre, screening, coefficients, occ_pattern):
    nocc = coefficients.shape[1]
    norb = coefficients.shape[0]
    bf, f32 = jnp.bfloat16, jnp.float32
    dma = pltpu.SemaphoreType.DMA
    vmem = pltpu.VMEM
    return pl.pallas_call(
        kernel,
        out_shape=jax.ShapeDtypeStruct((BLK, norb), f32),
        in_specs=[
            pl.BlockSpec(memory_space=pl.ANY),
            pl.BlockSpec(memory_space=vmem),
            pl.BlockSpec(memory_space=pl.ANY),
            pl.BlockSpec(memory_space=vmem),
        ],
        out_specs=pl.BlockSpec(memory_space=vmem),
        scratch_shapes=[
            vmem((4, BLK, norb), bf),
            vmem((norb, nocc), bf),
            vmem((2, 2, 2, BLK, nocc), bf),
            vmem((2, 7, BLK, nocc), bf),
            vmem((3, 2, 3, BLK, BLK), f32),
            vmem((3, 3, BLK, BLK), f32),
            vmem((3, X - 1, 2, 3, 32, BLK), f32),
            vmem((3, 2, 3, 32, BLK), f32),
            vmem((3, Z - 1, 16, BLK), f32),
            vmem((3, 16, BLK), f32),
            vmem((3, 16, BLK), f32),
            vmem((3, 16, BLK), f32),
            vmem((3, 2, 3, BLK, BLK), f32),
            dma((8,)),
            dma((2, 2)), dma((2, 2)),
            dma((2, 7)), dma((2, 7)),
            dma((3,)), dma((3,)),
            dma((3,)), dma((3,)),
            dma((3,)), dma((3,)),
            dma((3,)), dma((3,)),
            dma((3,)), dma((3,)),
            dma((3,)), dma((3,)),
        ],
        compiler_params=pltpu.CompilerParams(
            collective_id=0, has_side_effects=True, vmem_limit_bytes=48 * 2**20),
        cost_estimate=pl.CostEstimate(flops=3 * 10**9, bytes_accessed=6 * 10**6, transcendentals=0),
    )(three_centre, screening, coefficients, occ_pattern)


def solution(mesh):
    return jax.shard_map(
        on_device,
        mesh=mesh,
        in_specs=(P("aux", "orb", None), P("aux", "orb", None), P(), P()),
        out_specs=P("orb", None),
        check_vma=False,
    )
```

time: 353 us -> 104 us (0.29)
  the two profiles are of different devices: /device:TPU:1 before, /device:TPU:16 now
where the time goes in v1:
time: 104 us
  Pallas kernels  99.9 us (96%)
  local copies, waits for them, and re-layouts  3.94 us (4%)
    pallas_call x1, Pallas kernels, on_device(): pl.pallas_call(kernel, out_shape=jax.ShapeDtypeStruct((BLK, norb), f32),...  99.9 us
    unnamed x7, local copies, waits for them, and re-layouts  3.94 us

profile of v1, /device:TPU:16, one launch (start us, length us, event | category | flops | bytes accessed | tf_op | source)
XLA Modules:
  0.0 103.9 jit_solution(5889773893997600432)
XLA Ops:
  0.0 0.0 copy-start
  0.0 1.6 %copy-done = bf16[4,128,2048]{2,1,0:T(8,128)(2,1)S(1)} copy-done((bf16[4,128,2048]{2,1,0:T(8,128)(2,1)S(1)}, bf16[4,128,2048]{2,1,0:T(8,128)(2,1)}, u32[]{:S(2)}) %copy-start) | copy-done | bytes 2097176
  1.6 0.0 copy-start.1
  1.6 0.7 copy-done.1
  2.3 0.0 copy-start.2
  2.3 0.7 copy-done.2
  3.0 99.9 %shard_map.46 = f32[128,2048]{1,0:T(8,128)S(1)} custom-call(bf16[4,128,2048]{2,1,0:T(8,128)(2,1)S(1)} %copy-done, s32[4,1,16]{2,1,0:T(1,128)S(1)} %copy-done.2, bf16[2048,768]{1,0:T(8,128)(2,1)} %c_hbm.1, s32[16,48]{1,0:T(8,128)S(1)} %copy-done.1), custom_call_target="tpu_custom_call" | custom-call | flops 3000000000 | bytes 6000000 | tf_op jit(solution)/shard_map/pallas_call | solution.py:324
  102.9 1.0 copy.6
Async XLA Ops:
  0.0 1.6 %copy-start = (bf16[4,128,2048]{2,1,0:T(8,128)(2,1)S(1)}, bf16[4,128,2048]{2,1,0:T(8,128)(2,1)}, u32[]{:S(2)}) copy-start(bf16[4,128,2048]{2,1,0:T(8,128)(2,1)} %t_hbm.1) | copy-start | bytes 6291460
  1.6 0.7 copy-start.1
  2.3 0.7 copy-start.2

commit v2 on v1

v2 whole, which is shorter than its diff:
```python
import jax
import jax.numpy as jnp
from jax import lax
from jax.experimental import pallas as pl
from jax.experimental.pallas import tpu as pltpu
from jax.sharding import PartitionSpec as P

MESH = pl.DeviceIdType.MESH
X, Y, Z = 4, 8, 12
BLK = 128
NT = (((1,), (1,)), ((), ()))


SIGNS = (3, 2, 2, 1)
TILE = (16, 16, 16, 8)
OWNERS = (12, 8, 8, 8)
GROUPS = len(SIGNS)
QUART = BLK // X


def kernel(t_hbm, scr_hbm, c_hbm, occ_hbm, out_ref,
           tv, cv, scr_ref, occ_ref, h, ring,
           blk0, blk1, blk2, blk3, far0, far1, far2, far3,
           xa0, xa1, xa2, xa3, xb0, xb1, xb2, xb3, xs0, xs1, xs2, xs3,
           zr0, zr1, zr2, zr3, zt0, zt1, zt2, zt3, ze0, ze1, ze2, ze3,
           full0, full1, full2, full3,
           load_sem, part_s, part_r, ring_s, ring_r,
           xs_s, xs_r, xt_s, xt_r, zs_s, zs_r, e_s, e_r, zg_s, zg_r, xg_s, xg_r):
    blk, far = (blk0, blk1, blk2, blk3), (far0, far1, far2, far3)
    xa, xb, xs = (xa0, xa1, xa2, xa3), (xb0, xb1, xb2, xb3), (xs0, xs1, xs2, xs3)
    zr, zt, ze = (zr0, zr1, zr2, zr3), (zt0, zt1, zt2, zt3), (ze0, ze1, ze2, ze3)
    full = (full0, full1, full2, full3)
    aux = lax.axis_index("aux")
    orb = lax.axis_index("orb")
    x, z = aux // Z, aux % Z
    y, core = orb // 2, orb % 2
    other = 1 - core
    high = y // 4
    nocc = cv.shape[1]

    def dev(xx, zz, yy, cc):
        return (xx * Z + zz, yy * 2 + cc)

    def remote(src, dst, s_sem, r_sem, where):
        return pltpu.make_async_remote_copy(
            src_ref=src, dst_ref=dst, send_sem=s_sem, recv_sem=r_sem,
            device_id=where, device_id_type=MESH)

    partner = dev(x, z, y, other)
    nexts = (dev(x, z, (y + Y - 1) % Y, core), dev(x, z, (y + 1) % Y, core))

    def tile_of(g, zz):
        if g == 3:
            return 0, (zz // 4 + core) % 2, (zz % 4) * TILE[g]
        a, b, part = zz // 4, (zz // 2) % 2, zz % 2
        flip = (a + (y // 2 if g == 1 else y)) % 2
        sign = (1 - a // 2) * flip + (a // 2) * 2 if g == 0 else flip
        return sign, (b + core) % 2, part * TILE[g]

    def mirror(g):
        sign, k, _ = tile_of(g, z)
        dy = 4 if g == 3 else (1 - sign) * (g + 1) + sign * (Y - g - 1)
        return dev(x, z, (y + dy) % Y, k)

    def x_peer(d, cc):
        return dev((x + d) % X, z, y, cc)

    def z_peer(d):
        return dev(x, (z + d) % Z, y, core)

    def load_t(p):
        return pltpu.make_async_copy(t_hbm.at[p], tv.at[p], load_sem.at[p])

    crows = cv.shape[0] // 4

    def load_c(q):
        rows = pl.ds(q * crows, crows)
        return pltpu.make_async_copy(c_hbm.at[rows], cv.at[rows], load_sem.at[4 + q])

    load_occ = pltpu.make_async_copy(occ_hbm, occ_ref, load_sem.at[8])
    load_scr = pltpu.make_async_copy(scr_hbm, scr_ref, load_sem.at[9])
    load_occ.start()
    load_scr.start()
    for q in range(4):
        load_c(q).start()
    for p in range(4):
        load_t(p).start()

    barrier = pltpu.get_barrier_semaphore()

    def signal(where):
        pl.semaphore_signal(barrier, inc=1, device_id=where, device_id_type=MESH)

    signal(partner)
    signal(nexts[0])
    signal(nexts[1])
    for d in range(X):
        if d:
            signal(x_peer(d, core))
            signal(x_peer(d, other))

    @pl.loop(1, Z)
    def _(d):
        signal(z_peer(d))

    @pl.when(z < 8)
    def _():
        for g in range(GROUPS):
            signal(mirror(g))

    load_occ.wait()
    load_scr.wait()
    occ = occ_ref[...].astype(jnp.float32).astype(jnp.bfloat16)
    nslices = occ.shape[1]
    spread = (lax.broadcasted_iota(jnp.int32, (nslices, nocc), 1) // (nocc // nslices)
              == lax.broadcasted_iota(jnp.int32, (nslices, nocc), 0)).astype(jnp.float32).astype(jnp.bfloat16)
    occ_mask = jnp.dot(occ, spread, preferred_element_type=jnp.float32).astype(jnp.bfloat16)
    screen = scr_ref[...].reshape(4, 16).astype(jnp.float32).astype(jnp.bfloat16)
    widen = (lax.broadcasted_iota(jnp.int32, (16, 2048), 1) // BLK
             == lax.broadcasted_iota(jnp.int32, (16, 2048), 0)).astype(jnp.float32).astype(jnp.bfloat16)
    scr_mask = jnp.dot(screen, widen, preferred_element_type=jnp.float32).astype(jnp.bfloat16)

    for q in range(4):
        load_c(q).wait()
        for nb in range(4 * q, 4 * q + 4):
            rows = slice(nb * BLK, (nb + 1) * BLK)
            cv[rows, :] = cv[rows, :] * occ_mask[nb:nb + 1, :]

    for p in range(4):
        load_t(p).wait()
        tv[p] = tv[p] * scr_mask[p:p + 1, :]

    pl.semaphore_wait(barrier, 24 - 4 * (z // 8))

    def hop(d, slot):
        if slot < 2:
            src = h.at[core, slot, d]
        elif slot < 6:
            src = ring.at[d, slot - 2]
        else:
            target = (y + Y - 1) % Y if d == 0 else (y + 1) % Y
            src = ring.at[d, 4 + target // 4]
        return remote(src, ring.at[d, slot], ring_s.at[d, slot], ring_r.at[d, slot], nexts[d])

    def to_partner(t, d):
        return remote(h.at[core, t, d], h.at[core, t, d], part_s.at[t, d], part_r.at[t, d], partner)

    for t in range(2):
        lhs = tv[2 * t:2 * t + 2].reshape(2 * BLK, tv.shape[2])
        for n in range(nocc // 256):
            cols = slice(n * 256, (n + 1) * 256)
            r = jnp.dot(lhs, cv[:, cols], preferred_element_type=jnp.float32).astype(jnp.bfloat16)
            h[core, t, 0, :, cols] = r[:BLK]
            h[core, t, 1, :, cols] = r[BLK:]
        for d in range(2):
            hop(d, t).start()
        for d in range(2):
            to_partner(t, d).start()

    def dot_nt(a, b):
        return lax.dot_general(a, b, NT, preferred_element_type=jnp.float32)

    for t in range(2):
        for d in range(2):
            to_partner(t, d).wait_recv()
    for who, put in ((core, blk0), (other, far0)):
        total = None
        for t in range(2):
            for d in range(2):
                v = dot_nt(h[who, t, d], h[core, t, d])
                total = v if total is None else total + v
        put[2] = total

    def pair(who, t, d, slot, rows_own):
        a, b = h[who, t, d], ring[d, slot]
        return dot_nt(a, b) if rows_own else dot_nt(b, a)

    def ring_step(s, t):
        slot = 2 * (s - 1) + t
        for d in range(2):
            hop(d, slot).wait_recv()
            if slot < 4:
                hop(d, slot + 2).start()
            elif slot == 5:
                hop(d, 6).start()
        for d in range(2):
            own = pair(core, t, d, slot, d == 0)
            away = pair(other, t, d, slot, d == 0)
            if t == 0:
                blk[s - 1][d] = own
                far[s - 1][d] = away
            else:
                blk[s - 1][d] += own
                far[s - 1][d] += away

    def antipode():
        for d in range(2):
            hop(d, 6).wait_recv()

        for side in range(2):
            @pl.when(high == side)
            def _():
                blk[3][0] = pair(core, side, 0, 6, side == 0) + pair(core, side, 1, 6, side == 0)
                far[3][0] = pair(other, side, 0, 6, side == 0) + pair(other, side, 1, 6, side == 0)

    def wait_bytes(ref, sem):
        pltpu.make_async_copy(ref, ref, sem).wait()

    def quarter(xx):
        return pl.ds(pl.multiple_of(xx * QUART, QUART), QUART)

    def when_owner(g, fn):
        if OWNERS[g] == Z:
            fn()
        else:
            pl.when(z < OWNERS[g])(fn)

    def when_mirrored(fn):
        pl.when(z < 8)(fn)

    def xrs_start(g):
        for d in range(X):
            q = quarter((x + d) % X)
            if d:
                remote(blk[g].at[:, q, :], xa[g].at[d - 1], xs_s.at[g], xs_r.at[g], x_peer(d, core)).start()
            remote(far[g].at[:, q, :], xb[g].at[d], xt_s.at[g], xt_r.at[g], x_peer(d, other)).start()

    def tile(ref, g, zz, first=0):
        sign, k, row = tile_of(g, zz)
        return ref.at[k, sign, pl.ds(pl.multiple_of(first + row, TILE[g]), TILE[g]), :]

    def zrs_start(g):
        wait_bytes(xa[g], xs_r.at[g])
        wait_bytes(xb[g], xt_r.at[g])
        xs[g][core] = (blk[g][:, quarter(x), :] + xa[g][0]) + (xa[g][1] + xa[g][2])
        xs[g][other] = (xb[g][0] + xb[g][1]) + (xb[g][2] + xb[g][3])

        @pl.loop(1, Z)
        def _(d):
            zz = (z + d) % Z

            def send():
                remote(tile(xs[g], g, zz), zr[g].at[d - 1], zs_s.at[g], zs_r.at[g], z_peer(d)).start()

            if OWNERS[g] == Z:
                send()
            else:
                pl.when(zz < OWNERS[g])(send)

    def exchange(g):
        return remote(zt[g], ze[g], e_s.at[g], e_r.at[g], mirror(g))

    def ex_start(g):
        def collect():
            wait_bytes(zr[g], zs_r.at[g])
            total = tile(xs[g], g, z)[...]
            for d in range(Z - 1):
                total = total + zr[g][d]
            zt[g][...] = total

        when_owner(g, collect)
        when_mirrored(lambda: exchange(g).start())

    def zag_start(g):
        @pl.when(z < 8)
        def _():
            exchange(g).wait_recv()
            tile(full[g], g, z, x * QUART)[...] = zt[g][...] + ze[g][...]

        if g == 0:
            @pl.when(z >= 8)
            def _():
                tile(full[g], g, z, x * QUART)[...] = zt[g][...]

        def spread_out():
            @pl.loop(1, Z)
            def _(d):
                mine = tile(full[g], g, z, x * QUART)
                remote(mine, mine, zg_s.at[g], zg_r.at[g], z_peer(d)).start()

        when_owner(g, spread_out)

    def x_slab(g):
        return full[g].at[:, :, quarter(x), :]

    def three_quarters(g):
        return full[g].at[:, :, pl.ds(0, 3 * QUART), :]

    def xag_start(g):
        if OWNERS[g] == Z:
            wait_bytes(zr[g], zg_r.at[g])
        else:
            @pl.when(z < OWNERS[g])
            def _():
                wait_bytes(zr[g].at[pl.ds(0, OWNERS[g] - 1)], zg_r.at[g])

            @pl.when(z >= OWNERS[g])
            def _():
                wait_bytes(zr[g].at[pl.ds(0, OWNERS[g])], zg_r.at[g])
        for d in range(1, X):
            remote(x_slab(g), x_slab(g), xg_s.at[g], xg_r.at[g], x_peer(d, core)).start()

    def put(d, k, value):
        out_ref[:, pl.ds(pl.multiple_of((2 * d + k) * BLK, BLK), BLK)] = value

    def finish(g):
        wait_bytes(three_quarters(g), xg_r.at[g])
        s = g + 1
        if g < 3:
            for k in range(2):
                put((y + s) % Y, k, full[g][k, 0])
                put((y + Y - s) % Y, k, full[g][k, 1].T)
                if g == 0:
                    put(y, k, full[g][k, 2])
        else:
            for side in range(2):
                @pl.when(high == side)
                def _():
                    for k in range(2):
                        v = full[g][k, 0]
                        put((y + 4) % Y, k, v if side == 0 else v.T)

    ring_step(1, 0)
    ring_step(1, 1)
    xrs_start(0)
    ring_step(2, 0)
    ring_step(2, 1)
    xrs_start(1)
    zrs_start(0)
    ring_step(3, 0)
    ring_step(3, 1)
    xrs_start(2)
    ex_start(0)
    zrs_start(1)
    antipode()
    xrs_start(3)
    zag_start(0)
    ex_start(1)
    zrs_start(2)
    zrs_start(3)
    xag_start(0)
    zag_start(1)
    ex_start(2)
    ex_start(3)
    xag_start(1)
    finish(0)
    zag_start(2)
    zag_start(3)
    finish(1)
    xag_start(2)
    xag_start(3)
    finish(2)
    finish(3)

    for t in range(2):
        for d in range(2):
            to_partner(t, d).wait_send()
    for d in range(2):
        for slot in range(7):
            hop(d, slot).wait_send()
    for g in range(GROUPS):
        wait_bytes(xa[g], xs_s.at[g])
        wait_bytes(xb[g], xt_s.at[g])
        if OWNERS[g] == Z:
            wait_bytes(zr[g], zs_s.at[g])
            wait_bytes(zr[g], zg_s.at[g])
        else:
            @pl.when(z < OWNERS[g])
            def _():
                wait_bytes(zr[g].at[pl.ds(0, OWNERS[g] - 1)], zs_s.at[g])
                wait_bytes(zr[g], zg_s.at[g])

            @pl.when(z >= OWNERS[g])
            def _():
                wait_bytes(zr[g].at[pl.ds(0, OWNERS[g])], zs_s.at[g])
        when_mirrored(lambda: exchange(g).wait_send())
        wait_bytes(three_quarters(g), xg_s.at[g])


def on_device(three_centre, screening, coefficients, occ_pattern):
    nocc = coefficients.shape[1]
    norb = coefficients.shape[0]
    bf, f32 = jnp.bfloat16, jnp.float32
    dma = pltpu.SemaphoreType.DMA
    vmem = pltpu.VMEM
    return pl.pallas_call(
        kernel,
        out_shape=jax.ShapeDtypeStruct((BLK, norb), f32),
        in_specs=[pl.BlockSpec(memory_space=pl.ANY)] * 4,
        out_specs=pl.BlockSpec(memory_space=vmem),
        scratch_shapes=[
            vmem((4, BLK, norb), bf),
            vmem((norb, nocc), bf),
            vmem(screening.shape, jnp.int32),
            vmem(occ_pattern.shape, jnp.int32),
            vmem((2, 2, 2, BLK, nocc), bf),
            vmem((2, 7, BLK, nocc), bf),
            *[vmem((n, BLK, BLK), f32) for n in SIGNS],
            *[vmem((n, BLK, BLK), f32) for n in SIGNS],
            *[vmem((X - 1, n, QUART, BLK), f32) for n in SIGNS],
            *[vmem((X, n, QUART, BLK), f32) for n in SIGNS],
            *[vmem((2, n, QUART, BLK), f32) for n in SIGNS],
            *[vmem((Z - 1, r, BLK), f32) for r in TILE],
            *[vmem((r, BLK), f32) for r in TILE],
            *[vmem((r, BLK), f32) for r in TILE],
            *[vmem((2, n, BLK, BLK), f32) for n in SIGNS],
            dma((10,)),
            dma((2, 2)), dma((2, 2)),
            dma((2, 7)), dma((2, 7)),
            *[dma((GROUPS,))] * 12,
        ],
        compiler_params=pltpu.CompilerParams(
            collective_id=0, has_side_effects=True, vmem_limit_bytes=60 * 2**20),
        cost_estimate=pl.CostEstimate(flops=3 * 10**9, bytes_accessed=6 * 10**6, transcendentals=0),
    )(three_centre, screening, coefficients, occ_pattern)


def solution(mesh):
    return jax.shard_map(
        on_device,
        mesh=mesh,
        in_specs=(P("aux", "orb", None), P("aux", "orb", None), P(), P()),
        out_specs=P("orb", None),
        check_vma=False,
    )
```

time: 104 us -> 84.9 us (0.82)
  the two profiles are of different devices: /device:TPU:16 before, /device:TPU:1 now
where the time goes in v2:
time: 84.9 us; the launch traced here: 83.5 us
  Pallas kernels  81.2 us (96%)
  local copies, waits for them, and re-layouts  2.3 us (3%)
    pallas_call x1, Pallas kernels, on_device(): pl.pallas_call(kernel, out_shape=jax.ShapeDtypeStruct((BLK, norb), f32),...  81.2 us
    unnamed x1, local copies, waits for them, and re-layouts  2.3 us

profile of v2, /device:TPU:1, one launch (start us, length us, event | category | flops | bytes accessed | tf_op | source)
XLA Modules:
  0.0 83.5 jit_solution(11628612508942083597)
XLA Ops:
  0.0 81.2 %shard_map.46 = f32[128,2048]{1,0:T(8,128)} custom-call(bf16[4,128,2048]{2,1,0:T(8,128)(2,1)} %t_hbm.1, s32[4,1,16]{2,1,0:T(1,128)} %scr_hbm.1, bf16[2048,768]{1,0:T(8,128)(2,1)} %c_hbm.1, s32[16,48]{1,0:T(8,128)} %occ_hbm.1), custom_call_target="tpu_custom_call" | custom-call | flops 3000000000 | bytes 6000000 | tf_op jit(solution)/shard_map/pallas_call | solution.py:386
  81.2 2.3 %copy.6 = f32[128,2048]{1,0:T(8,128)} copy(f32[128,2048]{1,0:T(8,128)} %shard_map.46) | data formatting | bytes 2097152

commit v3 on v2

--- a/solution.py
+++ b/solution.py
@@ -25,7 +25,7 @@
            zr0, zr1, zr2, zr3, zt0, zt1, zt2, zt3, ze0, ze1, ze2, ze3,
            full0, full1, full2, full3,
            load_sem, part_s, part_r, ring_s, ring_r,
-           xs_s, xs_r, xt_s, xt_r, zs_s, zs_r, e_s, e_r, zg_s, zg_r, xg_s, xg_r):
+           xs_s, xs_r, xt_s, xt_r, zs_s, zs_r, e_s, e_r, zg_s, zg_r, xg_s, xh_s, xg_r):
     blk, far = (blk0, blk1, blk2, blk3), (far0, far1, far2, far3)
     xa, xb, xs = (xa0, xa1, xa2, xa3), (xb0, xb1, xb2, xb3), (xs0, xs1, xs2, xs3)
     zr, zt, ze = (zr0, zr1, zr2, zr3), (zt0, zt1, zt2, zt3), (ze0, ze1, ze2, ze3)
@@ -126,12 +126,6 @@
             rows = slice(nb * BLK, (nb + 1) * BLK)
             cv[rows, :] = cv[rows, :] * occ_mask[nb:nb + 1, :]
 
-    for p in range(4):
-        load_t(p).wait()
-        tv[p] = tv[p] * scr_mask[p:p + 1, :]
-
-    pl.semaphore_wait(barrier, 24 - 4 * (z // 8))
-
     def hop(d, slot):
         if slot < 2:
             src = h.at[core, slot, d]
@@ -146,12 +140,17 @@
         return remote(h.at[core, t, d], h.at[core, t, d], part_s.at[t, d], part_r.at[t, d], partner)
 
     for t in range(2):
+        for p in (2 * t, 2 * t + 1):
+            load_t(p).wait()
+            tv[p] = tv[p] * scr_mask[p:p + 1, :]
         lhs = tv[2 * t:2 * t + 2].reshape(2 * BLK, tv.shape[2])
         for n in range(nocc // 256):
             cols = slice(n * 256, (n + 1) * 256)
             r = jnp.dot(lhs, cv[:, cols], preferred_element_type=jnp.float32).astype(jnp.bfloat16)
             h[core, t, 0, :, cols] = r[:BLK]
             h[core, t, 1, :, cols] = r[BLK:]
+        if t == 0:
+            pl.semaphore_wait(barrier, 24 - 4 * (z // 8))
         for d in range(2):
             hop(d, t).start()
         for d in range(2):
@@ -297,14 +296,35 @@
             @pl.when(z >= OWNERS[g])
             def _():
                 wait_bytes(zr[g].at[pl.ds(0, OWNERS[g])], zg_r.at[g])
-        for d in range(1, X):
-            remote(x_slab(g), x_slab(g), xg_s.at[g], xg_r.at[g], x_peer(d, core)).start()
+        if g == 3:
+            for d in range(1, X):
+                remote(x_slab(g), x_slab(g), xg_s.at[g], xg_r.at[g, 0], x_peer(d, core)).start()
+        else:
+            for side in range(2):
+                x_first(g, side).start()
+
+    def x_first(g, side):
+        return remote(x_slab(g), x_slab(g), xg_s.at[g], xg_r.at[g, side], x_peer(X - 1 if side else 1, core))
+
+    def x_second(g, side):
+        start = ((x + (1 if side else X - 1)) % X) * QUART + side * (QUART // 2)
+        part = full[g].at[:, :, pl.ds(pl.multiple_of(start, QUART // 2), QUART // 2), :]
+        return remote(part, part, xh_s.at[g], xg_r.at[g, 2 + side], x_peer(X - 1 if side else 1, core))
+
+    def xag_forward(g):
+        for side in range(2):
+            x_first(g, side).wait_recv()
+            x_second(g, side).start()
 
     def put(d, k, value):
         out_ref[:, pl.ds(pl.multiple_of((2 * d + k) * BLK, BLK), BLK)] = value
 
     def finish(g):
-        wait_bytes(three_quarters(g), xg_r.at[g])
+        if g == 3:
+            wait_bytes(three_quarters(g), xg_r.at[g, 0])
+        else:
+            for side in range(2):
+                x_second(g, side).wait_recv()
         s = g + 1
         if g < 3:
             for k in range(2):
@@ -324,31 +344,34 @@
     ring_step(1, 1)
     xrs_start(0)
     ring_step(2, 0)
+    zrs_start(0)
     ring_step(2, 1)
     xrs_start(1)
-    zrs_start(0)
     ring_step(3, 0)
+    ex_start(0)
+    zrs_start(1)
     ring_step(3, 1)
     xrs_start(2)
-    ex_start(0)
-    zrs_start(1)
+    zag_start(0)
     antipode()
     xrs_start(3)
-    zag_start(0)
     ex_start(1)
+    xag_start(0)
     zrs_start(2)
+    zag_start(1)
     zrs_start(3)
-    xag_start(0)
-    zag_start(1)
+    xag_forward(0)
     ex_start(2)
+    xag_start(1)
     ex_start(3)
-    xag_start(1)
     finish(0)
     zag_start(2)
+    xag_forward(1)
     zag_start(3)
+    xag_start(2)
     finish(1)
-    xag_start(2)
     xag_start(3)
+    xag_forward(2)
     finish(2)
     finish(3)
 
@@ -374,7 +397,11 @@
             def _():
                 wait_bytes(zr[g].at[pl.ds(0, OWNERS[g])], zs_s.at[g])
         when_mirrored(lambda: exchange(g).wait_send())
-        wait_bytes(three_quarters(g), xg_s.at[g])
+        if g == 3:
+            wait_bytes(three_quarters(g), xg_s.at[g])
+        else:
+            wait_bytes(full[g].at[:, :, pl.ds(0, 2 * QUART), :], xg_s.at[g])
+            wait_bytes(full[g].at[:, :, pl.ds(0, QUART), :], xh_s.at[g])
 
 
 def on_device(three_centre, screening, coefficients, occ_pattern):
@@ -408,6 +435,7 @@
             dma((2, 2)), dma((2, 2)),
             dma((2, 7)), dma((2, 7)),
             *[dma((GROUPS,))] * 12,
+            dma((GROUPS, 4)),
         ],
         compiler_params=pltpu.CompilerParams(
             collective_id=0, has_side_effects=True, vmem_limit_bytes=60 * 2**20),

time: 84.9 us -> 83.2 us (0.980); the launches traced: 83.5 us -> 83 us
  no operation moved by 1% of the time
where the time goes in v3:
time: 83.2 us; the launch traced here: 83 us
  Pallas kernels  80.7 us (97%)
  local copies, waits for them, and re-layouts  2.3 us (3%)
    pallas_call x1, Pallas kernels, on_device(): pl.pallas_call(kernel, out_shape=jax.ShapeDtypeStruct((BLK, norb), f32),...  80.7 us
    unnamed x1, local copies, waits for them, and re-layouts  2.3 us

profile of v3, /device:TPU:1, one launch (start us, length us, event | category | flops | bytes accessed | tf_op | source)
XLA Modules:
  0.0 83.0 jit_solution(7875008480825755721)
XLA Ops:
  0.0 80.7 %shard_map.46 = f32[128,2048]{1,0:T(8,128)} custom-call(bf16[4,128,2048]{2,1,0:T(8,128)(2,1)} %t_hbm.1, s32[4,1,16]{2,1,0:T(1,128)} %scr_hbm.1, bf16[2048,768]{1,0:T(8,128)(2,1)} %c_hbm.1, s32[16,48]{1,0:T(8,128)} %occ_hbm.1), custom_call_target="tpu_custom_call" | custom-call | flops 3000000000 | bytes 6000000 | tf_op jit(solution)/shard_map/pallas_call | solution.py:413
  80.7 2.3 %copy.6 = f32[128,2048]{1,0:T(8,128)} copy(f32[128,2048]{1,0:T(8,128)} %shard_map.46) | data formatting | bytes 2097152

commit v4 on v2

--- a/solution.py
+++ b/solution.py
@@ -18,15 +18,15 @@
 QUART = BLK // X
 
 
-def kernel(t_hbm, scr_hbm, c_hbm, occ_hbm, out_ref,
-           tv, cv, scr_ref, occ_ref, h, ring,
-           blk0, blk1, blk2, blk3, far0, far1, far2, far3,
+def kernel(t_hbm, c_hbm, switch_ref, out_ref,
+           tv, cv, h, ring,
+           blk0, blk1, blk2, blk3,
            xa0, xa1, xa2, xa3, xb0, xb1, xb2, xb3, xs0, xs1, xs2, xs3,
            zr0, zr1, zr2, zr3, zt0, zt1, zt2, zt3, ze0, ze1, ze2, ze3,
            full0, full1, full2, full3,
            load_sem, part_s, part_r, ring_s, ring_r,
            xs_s, xs_r, xt_s, xt_r, zs_s, zs_r, e_s, e_r, zg_s, zg_r, xg_s, xg_r):
-    blk, far = (blk0, blk1, blk2, blk3), (far0, far1, far2, far3)
+    blk = (blk0, blk1, blk2, blk3)
     xa, xb, xs = (xa0, xa1, xa2, xa3), (xb0, xb1, xb2, xb3), (xs0, xs1, xs2, xs3)
     zr, zt, ze = (zr0, zr1, zr2, zr3), (zt0, zt1, zt2, zt3), (ze0, ze1, ze2, ze3)
     full = (full0, full1, full2, full3)
@@ -77,10 +77,6 @@
         rows = pl.ds(q * crows, crows)
         return pltpu.make_async_copy(c_hbm.at[rows], cv.at[rows], load_sem.at[4 + q])
 
-    load_occ = pltpu.make_async_copy(occ_hbm, occ_ref, load_sem.at[8])
-    load_scr = pltpu.make_async_copy(scr_hbm, scr_ref, load_sem.at[9])
-    load_occ.start()
-    load_scr.start()
     for q in range(4):
         load_c(q).start()
     for p in range(4):
@@ -108,14 +104,13 @@
         for g in range(GROUPS):
             signal(mirror(g))
 
-    load_occ.wait()
-    load_scr.wait()
-    occ = occ_ref[...].astype(jnp.float32).astype(jnp.bfloat16)
+    switches = switch_ref[...]
+    occ = switches[:16].astype(jnp.float32).astype(jnp.bfloat16)
     nslices = occ.shape[1]
     spread = (lax.broadcasted_iota(jnp.int32, (nslices, nocc), 1) // (nocc // nslices)
               == lax.broadcasted_iota(jnp.int32, (nslices, nocc), 0)).astype(jnp.float32).astype(jnp.bfloat16)
     occ_mask = jnp.dot(occ, spread, preferred_element_type=jnp.float32).astype(jnp.bfloat16)
-    screen = scr_ref[...].reshape(4, 16).astype(jnp.float32).astype(jnp.bfloat16)
+    screen = switches[16:20, :16].astype(jnp.float32).astype(jnp.bfloat16)
     widen = (lax.broadcasted_iota(jnp.int32, (16, 2048), 1) // BLK
              == lax.broadcasted_iota(jnp.int32, (16, 2048), 0)).astype(jnp.float32).astype(jnp.bfloat16)
     scr_mask = jnp.dot(screen, widen, preferred_element_type=jnp.float32).astype(jnp.bfloat16)
@@ -125,12 +120,6 @@
         for nb in range(4 * q, 4 * q + 4):
             rows = slice(nb * BLK, (nb + 1) * BLK)
             cv[rows, :] = cv[rows, :] * occ_mask[nb:nb + 1, :]
-
-    for p in range(4):
-        load_t(p).wait()
-        tv[p] = tv[p] * scr_mask[p:p + 1, :]
-
-    pl.semaphore_wait(barrier, 24 - 4 * (z // 8))
 
     def hop(d, slot):
         if slot < 2:
@@ -146,12 +135,17 @@
         return remote(h.at[core, t, d], h.at[core, t, d], part_s.at[t, d], part_r.at[t, d], partner)
 
     for t in range(2):
+        for p in (2 * t, 2 * t + 1):
+            load_t(p).wait()
+            tv[p] = tv[p] * scr_mask[p:p + 1, :]
         lhs = tv[2 * t:2 * t + 2].reshape(2 * BLK, tv.shape[2])
         for n in range(nocc // 256):
             cols = slice(n * 256, (n + 1) * 256)
             r = jnp.dot(lhs, cv[:, cols], preferred_element_type=jnp.float32).astype(jnp.bfloat16)
             h[core, t, 0, :, cols] = r[:BLK]
             h[core, t, 1, :, cols] = r[BLK:]
+        if t == 0:
+            pl.semaphore_wait(barrier, 24 - 4 * (z // 8))
         for d in range(2):
             hop(d, t).start()
         for d in range(2):
@@ -163,17 +157,24 @@
     for t in range(2):
         for d in range(2):
             to_partner(t, d).wait_recv()
-    for who, put in ((core, blk0), (other, far0)):
-        total = None
-        for t in range(2):
-            for d in range(2):
-                v = dot_nt(h[who, t, d], h[core, t, d])
-                total = v if total is None else total + v
-        put[2] = total
-
-    def pair(who, t, d, slot, rows_own):
-        a, b = h[who, t, d], ring[d, slot]
-        return dot_nt(a, b) if rows_own else dot_nt(b, a)
+    def chip_rows(t, d):
+        return h[:, t, d].reshape(2 * BLK, nocc)
+
+    total = None
+    for t in range(2):
+        for d in range(2):
+            v = dot_nt(chip_rows(t, d), h[core, t, d])
+            total = v if total is None else total + v
+    blk[0][0, 2] = total[:BLK]
+    blk[0][1, 2] = total[BLK:]
+
+    def pair(t, d, slot, rows_own):
+        a, b = chip_rows(t, d), ring[d, slot]
+        if rows_own:
+            r = dot_nt(a, b)
+            return r[:BLK], r[BLK:]
+        r = dot_nt(b, a)
+        return r[:, :BLK], r[:, BLK:]
 
     def ring_step(s, t):
         slot = 2 * (s - 1) + t
@@ -184,14 +185,12 @@
             elif slot == 5:
                 hop(d, 6).start()
         for d in range(2):
-            own = pair(core, t, d, slot, d == 0)
-            away = pair(other, t, d, slot, d == 0)
-            if t == 0:
-                blk[s - 1][d] = own
-                far[s - 1][d] = away
-            else:
-                blk[s - 1][d] += own
-                far[s - 1][d] += away
+            parts = pair(t, d, slot, d == 0)
+            for who in range(2):
+                if t == 0:
+                    blk[s - 1][who, d] = parts[who]
+                else:
+                    blk[s - 1][who, d] += parts[who]
 
     def antipode():
         for d in range(2):
@@ -200,8 +199,10 @@
         for side in range(2):
             @pl.when(high == side)
             def _():
-                blk[3][0] = pair(core, side, 0, 6, side == 0) + pair(core, side, 1, 6, side == 0)
-                far[3][0] = pair(other, side, 0, 6, side == 0) + pair(other, side, 1, 6, side == 0)
+                left = pair(side, 0, 6, side == 0)
+                right = pair(side, 1, 6, side == 0)
+                for who in range(2):
+                    blk[3][who, 0] = left[who] + right[who]
 
     def wait_bytes(ref, sem):
         pltpu.make_async_copy(ref, ref, sem).wait()
@@ -222,8 +223,8 @@
         for d in range(X):
             q = quarter((x + d) % X)
             if d:
-                remote(blk[g].at[:, q, :], xa[g].at[d - 1], xs_s.at[g], xs_r.at[g], x_peer(d, core)).start()
-            remote(far[g].at[:, q, :], xb[g].at[d], xt_s.at[g], xt_r.at[g], x_peer(d, other)).start()
+                remote(blk[g].at[core, :, q, :], xa[g].at[d - 1], xs_s.at[g], xs_r.at[g], x_peer(d, core)).start()
+            remote(blk[g].at[other, :, q, :], xb[g].at[d], xt_s.at[g], xt_r.at[g], x_peer(d, other)).start()
 
     def tile(ref, g, zz, first=0):
         sign, k, row = tile_of(g, zz)
@@ -232,7 +233,7 @@
     def zrs_start(g):
         wait_bytes(xa[g], xs_r.at[g])
         wait_bytes(xb[g], xt_r.at[g])
-        xs[g][core] = (blk[g][:, quarter(x), :] + xa[g][0]) + (xa[g][1] + xa[g][2])
+        xs[g][core] = (blk[g][core, :, quarter(x), :] + xa[g][0]) + (xa[g][1] + xa[g][2])
         xs[g][other] = (xb[g][0] + xb[g][1]) + (xb[g][2] + xb[g][3])
 
         @pl.loop(1, Z)
@@ -324,27 +325,27 @@
     ring_step(1, 1)
     xrs_start(0)
     ring_step(2, 0)
+    zrs_start(0)
     ring_step(2, 1)
     xrs_start(1)
-    zrs_start(0)
     ring_step(3, 0)
+    ex_start(0)
+    zrs_start(1)
     ring_step(3, 1)
     xrs_start(2)
-    ex_start(0)
-    zrs_start(1)
+    zag_start(0)
     antipode()
     xrs_start(3)
-    zag_start(0)
     ex_start(1)
     zrs_start(2)
-    zrs_start(3)
     xag_start(0)
     zag_start(1)
+    zrs_start(3)
     ex_start(2)
+    xag_start(1)
+    zag_start(2)
     ex_start(3)
-    xag_start(1)
     finish(0)
-    zag_start(2)
     zag_start(3)
     finish(1)
     xag_start(2)
@@ -383,20 +384,20 @@
     bf, f32 = jnp.bfloat16, jnp.float32
     dma = pltpu.SemaphoreType.DMA
     vmem = pltpu.VMEM
+    nslices = occ_pattern.shape[1]
+    switches = jnp.concatenate(
+        [occ_pattern, jnp.pad(screening[:, 0, :], ((0, 4), (0, nslices - screening.shape[2])))], axis=0)
     return pl.pallas_call(
         kernel,
         out_shape=jax.ShapeDtypeStruct((BLK, norb), f32),
-        in_specs=[pl.BlockSpec(memory_space=pl.ANY)] * 4,
+        in_specs=[pl.BlockSpec(memory_space=pl.ANY)] * 2 + [pl.BlockSpec(memory_space=vmem)],
         out_specs=pl.BlockSpec(memory_space=vmem),
         scratch_shapes=[
             vmem((4, BLK, norb), bf),
             vmem((norb, nocc), bf),
-            vmem(screening.shape, jnp.int32),
-            vmem(occ_pattern.shape, jnp.int32),
             vmem((2, 2, 2, BLK, nocc), bf),
             vmem((2, 7, BLK, nocc), bf),
-            *[vmem((n, BLK, BLK), f32) for n in SIGNS],
-            *[vmem((n, BLK, BLK), f32) for n in SIGNS],
+            *[vmem((2, n, BLK, BLK), f32) for n in SIGNS],
             *[vmem((X - 1, n, QUART, BLK), f32) for n in SIGNS],
             *[vmem((X, n, QUART, BLK), f32) for n in SIGNS],
             *[vmem((2, n, QUART, BLK), f32) for n in SIGNS],
@@ -404,15 +405,15 @@
             *[vmem((r, BLK), f32) for r in TILE],
             *[vmem((r, BLK), f32) for r in TILE],
             *[vmem((2, n, BLK, BLK), f32) for n in SIGNS],
-            dma((10,)),
+            dma((8,)),
             dma((2, 2)), dma((2, 2)),
             dma((2, 7)), dma((2, 7)),
             *[dma((GROUPS,))] * 12,
         ],
         compiler_params=pltpu.CompilerParams(
-            collective_id=0, has_side_effects=True, vmem_limit_bytes=60 * 2**20),
+            collective_id=0, has_side_effects=True, vmem_limit_bytes=52 * 2**20),
         cost_estimate=pl.CostEstimate(flops=3 * 10**9, bytes_accessed=6 * 10**6, transcendentals=0),
-    )(three_centre, screening, coefficients, occ_pattern)
+    )(three_centre, coefficients, switches)
 
 
 def solution(mesh):

time: 84.9 us -> 79.9 us (0.941); the launches traced: 83.5 us -> 79.7 us
  Pallas kernels: 81.2 us -> 78 us
  local copies, waits for them, and re-layouts: 2.3 us -> 0.97 us
    pallas_call x1, Pallas kernels: 81.2 us -> 78 us  [on_device(): pl.pallas_call(kernel, out_shape=jax.ShapeDtypeStruct((BLK, norb), f32),...]
    unnamed x1, local copies, waits for them, and re-layouts: 2.3 us -> 0.97 us
where the time goes in v4:
time: 79.9 us; the launch traced here: 79.7 us
  Pallas kernels  78 us (98%)
  local copies, waits for them, and re-layouts  0.97 us (1%)
    pallas_call x1, Pallas kernels, on_device(): pl.pallas_call(kernel, out_shape=jax.ShapeDtypeStruct((BLK, norb), f32),...  78 us

profile of v4, /device:TPU:1, one launch (start us, length us, event | category | flops | bytes accessed | tf_op | source)
XLA Modules:
  0.0 79.7 jit_solution(1002400455860097671)
XLA Ops:
  0.0 0.7 pad_add_fusion.switch_ref
  0.7 78.0 %shard_map.46 = f32[128,2048]{1,0:T(8,128)S(1)} custom-call(bf16[4,128,2048]{2,1,0:T(8,128)(2,1)} %t_hbm.1, bf16[2048,768]{1,0:T(8,128)(2,1)} %c_hbm.1, s32[24,48]{1,0:T(8,128)S(1)} %pad_add_fusion.switch_ref), custom_call_target="tpu_custom_call" | custom-call | flops 3000000000 | bytes 6000000 | tf_op jit(solution)/shard_map/pallas_call | solution.py:390
  78.7 1.0 %copy.6 = f32[128,2048]{1,0:T(8,128)} copy(f32[128,2048]{1,0:T(8,128)S(1)} %shard_map.46) | data formatting | bytes 2097152

commit v5 on v4

--- a/solution.py
+++ b/solution.py
@@ -68,6 +68,9 @@
     def z_peer(d):
         return dev(x, (z + d) % Z, y, core)
 
+    def far_first(i):
+        return Z // 2 + (2 * (i % 2) - 1) * ((i + 1) // 2)
+
     def load_t(p):
         return pltpu.make_async_copy(t_hbm.at[p], tv.at[p], load_sem.at[p])
 
@@ -220,7 +223,7 @@
         pl.when(z < 8)(fn)
 
     def xrs_start(g):
-        for d in range(X):
+        for d in (2, 1, 3, 0):
             q = quarter((x + d) % X)
             if d:
                 remote(blk[g].at[core, :, q, :], xa[g].at[d - 1], xs_s.at[g], xs_r.at[g], x_peer(d, core)).start()
@@ -236,8 +239,9 @@
         xs[g][core] = (blk[g][core, :, quarter(x), :] + xa[g][0]) + (xa[g][1] + xa[g][2])
         xs[g][other] = (xb[g][0] + xb[g][1]) + (xb[g][2] + xb[g][3])
 
-        @pl.loop(1, Z)
-        def _(d):
+        @pl.loop(0, Z - 1)
+        def _(i):
+            d = far_first(i)
             zz = (z + d) % Z
 
             def send():
@@ -274,10 +278,10 @@
                 tile(full[g], g, z, x * QUART)[...] = zt[g][...]
 
         def spread_out():
-            @pl.loop(1, Z)
-            def _(d):
+            @pl.loop(0, Z - 1)
+            def _(i):
                 mine = tile(full[g], g, z, x * QUART)
-                remote(mine, mine, zg_s.at[g], zg_r.at[g], z_peer(d)).start()
+                remote(mine, mine, zg_s.at[g], zg_r.at[g], z_peer(far_first(i))).start()
 
         when_owner(g, spread_out)
 
@@ -298,7 +302,7 @@
             @pl.when(z >= OWNERS[g])
             def _():
                 wait_bytes(zr[g].at[pl.ds(0, OWNERS[g])], zg_r.at[g])
-        for d in range(1, X):
+        for d in (2, 1, 3):
             remote(x_slab(g), x_slab(g), xg_s.at[g], xg_r.at[g], x_peer(d, core)).start()
 
     def put(d, k, value):

time: 79.9 us -> 80.2 us (level)
  no operation moved by 1% of the time
where the time goes in v5:
time: 80.2 us; the launch traced here: 80 us
  Pallas kernels  78.3 us (98%)
  local copies, waits for them, and re-layouts  0.97 us (1%)
    pallas_call x1, Pallas kernels, on_device(): pl.pallas_call(kernel, out_shape=jax.ShapeDtypeStruct((BLK, norb), f32),...  78.3 us

profile of v5, /device:TPU:1, one launch (start us, length us, event | category | flops | bytes accessed | tf_op | source)
XLA Modules:
  0.0 80.0 jit_solution(62480425345407601)
XLA Ops:
  0.0 0.7 pad_add_fusion.switch_ref
  0.7 78.3 %shard_map.46 = f32[128,2048]{1,0:T(8,128)S(1)} custom-call(bf16[4,128,2048]{2,1,0:T(8,128)(2,1)} %t_hbm.1, bf16[2048,768]{1,0:T(8,128)(2,1)} %c_hbm.1, s32[24,48]{1,0:T(8,128)S(1)} %pad_add_fusion.switch_ref), custom_call_target="tpu_custom_call" | custom-call | flops 3000000000 | bytes 6000000 | tf_op jit(solution)/shard_map/pallas_call | solution.py:394
  79.0 1.0 %copy.6 = f32[128,2048]{1,0:T(8,128)} copy(f32[128,2048]{1,0:T(8,128)S(1)} %shard_map.46) | data formatting | bytes 2097152

commit v6 on v4

--- a/solution.py
+++ b/solution.py
@@ -14,6 +14,7 @@
 SIGNS = (3, 2, 2, 1)
 TILE = (16, 16, 16, 8)
 OWNERS = (12, 8, 8, 8)
+SOURCES = (Z - 1, Z - 1, Z - 1, 2 * Z - 1)
 GROUPS = len(SIGNS)
 QUART = BLK // X
 
@@ -22,13 +23,13 @@
            tv, cv, h, ring,
            blk0, blk1, blk2, blk3,
            xa0, xa1, xa2, xa3, xb0, xb1, xb2, xb3, xs0, xs1, xs2, xs3,
-           zr0, zr1, zr2, zr3, zt0, zt1, zt2, zt3, ze0, ze1, ze2, ze3,
+           zr0, zr1, zr2, zr3, zt0, zt1, zt2, zt3, ze0, ze1, ze2,
            full0, full1, full2, full3,
            load_sem, part_s, part_r, ring_s, ring_r,
            xs_s, xs_r, xt_s, xt_r, zs_s, zs_r, e_s, e_r, zg_s, zg_r, xg_s, xg_r):
     blk = (blk0, blk1, blk2, blk3)
     xa, xb, xs = (xa0, xa1, xa2, xa3), (xb0, xb1, xb2, xb3), (xs0, xs1, xs2, xs3)
-    zr, zt, ze = (zr0, zr1, zr2, zr3), (zt0, zt1, zt2, zt3), (ze0, ze1, ze2, ze3)
+    zr, zt, ze = (zr0, zr1, zr2, zr3), (zt0, zt1, zt2, zt3), (ze0, ze1, ze2)
     full = (full0, full1, full2, full3)
     aux = lax.axis_index("aux")
     orb = lax.axis_index("orb")
@@ -59,7 +60,7 @@
 
     def mirror(g):
         sign, k, _ = tile_of(g, z)
-        dy = 4 if g == 3 else (1 - sign) * (g + 1) + sign * (Y - g - 1)
+        dy = (1 - sign) * (g + 1) + sign * (Y - g - 1)
         return dev(x, z, (y + dy) % Y, k)
 
     def x_peer(d, cc):
@@ -101,15 +102,19 @@
 
     @pl.when(z < 8)
     def _():
-        for g in range(GROUPS):
+        for g in range(3):
             signal(mirror(g))
+
+        @pl.loop(0, Z)
+        def _(zz):
+            signal(dev(x, zz, (y + 4) % Y, (z // 4 + core) % 2))
 
     switches = switch_ref[...]
     occ = switches[:16].astype(jnp.float32).astype(jnp.bfloat16)
     nslices = occ.shape[1]
-    spread = (lax.broadcasted_iota(jnp.int32, (nslices, nocc), 1) // (nocc // nslices)
+    by_slice = (lax.broadcasted_iota(jnp.int32, (nslices, nocc), 1) // (nocc // nslices)
               == lax.broadcasted_iota(jnp.int32, (nslices, nocc), 0)).astype(jnp.float32).astype(jnp.bfloat16)
-    occ_mask = jnp.dot(occ, spread, preferred_element_type=jnp.float32).astype(jnp.bfloat16)
+    occ_mask = jnp.dot(occ, by_slice, preferred_element_type=jnp.float32).astype(jnp.bfloat16)
     screen = switches[16:20, :16].astype(jnp.float32).astype(jnp.bfloat16)
     widen = (lax.broadcasted_iota(jnp.int32, (16, 2048), 1) // BLK
              == lax.broadcasted_iota(jnp.int32, (16, 2048), 0)).astype(jnp.float32).astype(jnp.bfloat16)
@@ -145,7 +150,7 @@
             h[core, t, 0, :, cols] = r[:BLK]
             h[core, t, 1, :, cols] = r[BLK:]
         if t == 0:
-            pl.semaphore_wait(barrier, 24 - 4 * (z // 8))
+            pl.semaphore_wait(barrier, 31 - 3 * (z // 8))
         for d in range(2):
             hop(d, t).start()
         for d in range(2):
@@ -236,6 +241,12 @@
         xs[g][core] = (blk[g][core, :, quarter(x), :] + xa[g][0]) + (xa[g][1] + xa[g][2])
         xs[g][other] = (xb[g][0] + xb[g][1]) + (xb[g][2] + xb[g][3])
 
+        if g == 3:
+            @pl.loop(0, OWNERS[g])
+            def _(zz):
+                remote(tile(xs[g], g, zz), zr[g].at[Z - 1 + z], zs_s.at[g], zs_r.at[g],
+                       dev(x, zz, (y + 4) % Y, (zz // 4 + core) % 2)).start()
+
         @pl.loop(1, Z)
         def _(d):
             zz = (z + d) % Z
@@ -255,18 +266,22 @@
         def collect():
             wait_bytes(zr[g], zs_r.at[g])
             total = tile(xs[g], g, z)[...]
-            for d in range(Z - 1):
+            for d in range(SOURCES[g]):
                 total = total + zr[g][d]
             zt[g][...] = total
 
         when_owner(g, collect)
-        when_mirrored(lambda: exchange(g).start())
+        if g < 3:
+            when_mirrored(lambda: exchange(g).start())
 
     def zag_start(g):
         @pl.when(z < 8)
         def _():
-            exchange(g).wait_recv()
-            tile(full[g], g, z, x * QUART)[...] = zt[g][...] + ze[g][...]
+            total = zt[g][...]
+            if g < 3:
+                exchange(g).wait_recv()
+                total = total + ze[g][...]
+            tile(full[g], g, z, x * QUART)[...] = total
 
         if g == 0:
             @pl.when(z >= 8)
@@ -350,8 +365,6 @@
     finish(1)
     xag_start(2)
     xag_start(3)
-    finish(2)
-    finish(3)
 
     for t in range(2):
         for d in range(2):
@@ -362,19 +375,26 @@
     for g in range(GROUPS):
         wait_bytes(xa[g], xs_s.at[g])
         wait_bytes(xb[g], xt_s.at[g])
+        spread = zr[g].at[pl.ds(0, Z - 1)]
         if OWNERS[g] == Z:
-            wait_bytes(zr[g], zs_s.at[g])
-            wait_bytes(zr[g], zg_s.at[g])
+            wait_bytes(spread, zs_s.at[g])
+            wait_bytes(spread, zg_s.at[g])
         else:
+            sent = OWNERS[g] * (2 if g == 3 else 1)
+
             @pl.when(z < OWNERS[g])
             def _():
-                wait_bytes(zr[g].at[pl.ds(0, OWNERS[g] - 1)], zs_s.at[g])
-                wait_bytes(zr[g], zg_s.at[g])
+                wait_bytes(zr[g].at[pl.ds(0, sent - 1)], zs_s.at[g])
+                wait_bytes(spread, zg_s.at[g])
 
             @pl.when(z >= OWNERS[g])
             def _():
-                wait_bytes(zr[g].at[pl.ds(0, OWNERS[g])], zs_s.at[g])
-        when_mirrored(lambda: exchange(g).wait_send())
+                wait_bytes(zr[g].at[pl.ds(0, sent)], zs_s.at[g])
+        if g < 3:
+            when_mirrored(lambda: exchange(g).wait_send())
+    finish(2)
+    finish(3)
+    for g in range(GROUPS):
         wait_bytes(three_quarters(g), xg_s.at[g])
 
 
@@ -401,9 +421,9 @@
             *[vmem((X - 1, n, QUART, BLK), f32) for n in SIGNS],
             *[vmem((X, n, QUART, BLK), f32) for n in SIGNS],
             *[vmem((2, n, QUART, BLK), f32) for n in SIGNS],
-            *[vmem((Z - 1, r, BLK), f32) for r in TILE],
+            *[vmem((n, r, BLK), f32) for n, r in zip(SOURCES, TILE)],
             *[vmem((r, BLK), f32) for r in TILE],
-            *[vmem((r, BLK), f32) for r in TILE],
+            *[vmem((r, BLK), f32) for r in TILE[:3]],
             *[vmem((2, n, BLK, BLK), f32) for n in SIGNS],
             dma((8,)),
             dma((2, 2)), dma((2, 2)),

time: 79.9 us -> 84.2 us (1.054); the launches traced: 79.7 us -> 82.8 us
  Pallas kernels: 78 us -> 81.1 us
    pallas_call x1, Pallas kernels: 78 us -> 81.1 us  [on_device(): pl.pallas_call(kernel, out_shape=jax.ShapeDtypeStruct((BLK, norb), f32),...]
where the time goes in v6:
time: 84.2 us; the launch traced here: 82.8 us
  Pallas kernels  81.1 us (96%)
  local copies, waits for them, and re-layouts  0.97 us (1%)
    pallas_call x1, Pallas kernels, on_device(): pl.pallas_call(kernel, out_shape=jax.ShapeDtypeStruct((BLK, norb), f32),...  81.1 us

profile of v6, /device:TPU:1, one launch (start us, length us, event | category | flops | bytes accessed | tf_op | source)
XLA Modules:
  0.0 82.8 jit_solution(14801506254446434154)
XLA Ops:
  0.0 0.7 pad_add_fusion.switch_ref
  0.7 81.1 %shard_map.46 = f32[128,2048]{1,0:T(8,128)S(1)} custom-call(bf16[4,128,2048]{2,1,0:T(8,128)(2,1)} %t_hbm.1, bf16[2048,768]{1,0:T(8,128)(2,1)} %c_hbm.1, s32[24,48]{1,0:T(8,128)S(1)} %pad_add_fusion.switch_ref), custom_call_target="tpu_custom_call" | custom-call | flops 3000000000 | bytes 6000000 | tf_op jit(solution)/shard_map/pallas_call | solution.py:410
  81.9 1.0 %copy.6 = f32[128,2048]{1,0:T(8,128)} copy(f32[128,2048]{1,0:T(8,128)S(1)} %shard_map.46) | data formatting | bytes 2097152

commit v7 on v4

--- a/solution.py
+++ b/solution.py
@@ -69,7 +69,9 @@
         return dev(x, (z + d) % Z, y, core)
 
     def load_t(p):
-        return pltpu.make_async_copy(t_hbm.at[p], tv.at[p], load_sem.at[p])
+        f, d = p // 2, p % 2
+        source = 2 * ((f + 1 + high) % 2) + d
+        return pltpu.make_async_copy(t_hbm.at[source], tv.at[p], load_sem.at[p])
 
     crows = cv.shape[0] // 4
 
@@ -127,8 +129,7 @@
         elif slot < 6:
             src = ring.at[d, slot - 2]
         else:
-            target = (y + Y - 1) % Y if d == 0 else (y + 1) % Y
-            src = ring.at[d, 4 + target // 4]
+            src = ring.at[d, 4]
         return remote(src, ring.at[d, slot], ring_s.at[d, slot], ring_r.at[d, slot], nexts[d])
 
     def to_partner(t, d):
@@ -137,7 +138,9 @@
     for t in range(2):
         for p in (2 * t, 2 * t + 1):
             load_t(p).wait()
-            tv[p] = tv[p] * scr_mask[p:p + 1, :]
+            f, d = p // 2, p % 2
+            own_mask = jnp.where(high == 1 - f, scr_mask[d:d + 1, :], scr_mask[2 + d:3 + d, :])
+            tv[p] = tv[p] * own_mask
         lhs = tv[2 * t:2 * t + 2].reshape(2 * BLK, tv.shape[2])
         for n in range(nocc // 256):
             cols = slice(n * 256, (n + 1) * 256)
@@ -182,10 +185,11 @@
             hop(d, slot).wait_recv()
             if slot < 4:
                 hop(d, slot + 2).start()
-            elif slot == 5:
+            elif slot == 4:
                 hop(d, 6).start()
         for d in range(2):
-            parts = pair(t, d, slot, d == 0)
+            sender = (y + s) % Y if d == 0 else (y + Y - s) % Y
+            parts = pair((t + sender // 4 + high) % 2, d, slot, d == 0)
             for who in range(2):
                 if t == 0:
                     blk[s - 1][who, d] = parts[who]
@@ -199,8 +203,8 @@
         for side in range(2):
             @pl.when(high == side)
             def _():
-                left = pair(side, 0, 6, side == 0)
-                right = pair(side, 1, 6, side == 0)
+                left = pair(1, 0, 6, side == 0)
+                right = pair(1, 1, 6, side == 0)
                 for who in range(2):
                     blk[3][who, 0] = left[who] + right[who]
 

time: 79.9 us -> 81.4 us (1.019)
  Pallas kernels: 78 us -> 79.5 us
    pallas_call x1, Pallas kernels: 78 us -> 79.5 us  [on_device(): pl.pallas_call(kernel, out_shape=jax.ShapeDtypeStruct((BLK, norb), f32),...]
where the time goes in v7:
time: 81.4 us; the launch traced here: 81.2 us
  Pallas kernels  79.5 us (98%)
  local copies, waits for them, and re-layouts  0.97 us (1%)
    pallas_call x1, Pallas kernels, on_device(): pl.pallas_call(kernel, out_shape=jax.ShapeDtypeStruct((BLK, norb), f32),...  79.5 us

profile of v7, /device:TPU:1, one launch (start us, length us, event | category | flops | bytes accessed | tf_op | source)
XLA Modules:
  0.0 81.2 jit_solution(8461990897560501588)
XLA Ops:
  0.0 0.7 pad_add_fusion.switch_ref
  0.7 79.5 %shard_map.46 = f32[128,2048]{1,0:T(8,128)S(1)} custom-call(bf16[4,128,2048]{2,1,0:T(8,128)(2,1)} %t_hbm.1, bf16[2048,768]{1,0:T(8,128)(2,1)} %c_hbm.1, s32[24,48]{1,0:T(8,128)S(1)} %pad_add_fusion.switch_ref), custom_call_target="tpu_custom_call" | custom-call | flops 3000000000 | bytes 6000000 | tf_op jit(solution)/shard_map/pallas_call | solution.py:394
  80.2 1.0 %copy.6 = f32[128,2048]{1,0:T(8,128)} copy(f32[128,2048]{1,0:T(8,128)S(1)} %shard_map.46) | data formatting | bytes 2097152

commit v8 on v7

--- a/solution.py
+++ b/solution.py
@@ -25,7 +25,7 @@
            zr0, zr1, zr2, zr3, zt0, zt1, zt2, zt3, ze0, ze1, ze2, ze3,
            full0, full1, full2, full3,
            load_sem, part_s, part_r, ring_s, ring_r,
-           xs_s, xs_r, xt_s, xt_r, zs_s, zs_r, e_s, e_r, zg_s, zg_r, xg_s, xg_r):
+           xs_s, xs_r, xt_s, xt_r, zs_s, zs_r, e_s, e_r, zg_s, zg_r, xg_s, xg_r, known):
     blk = (blk0, blk1, blk2, blk3)
     xa, xb, xs = (xa0, xa1, xa2, xa3), (xb0, xb1, xb2, xb3), (xs0, xs1, xs2, xs3)
     zr, zt, ze = (zr0, zr1, zr2, zr3), (zt0, zt1, zt2, zt3), (ze0, ze1, ze2, ze3)
@@ -97,14 +97,15 @@
             signal(x_peer(d, core))
             signal(x_peer(d, other))
 
-    @pl.loop(1, Z)
-    def _(d):
-        signal(z_peer(d))
-
-    @pl.when(z < 8)
-    def _():
-        for g in range(GROUPS):
-            signal(mirror(g))
+    signal(z_peer(1))
+    signal(z_peer(Z - 1))
+
+    def tell(r):
+        for d in (2 ** r, Z - 2 ** r):
+            pl.semaphore_signal(known.at[r], inc=1, device_id=z_peer(d), device_id_type=MESH)
+
+    def hear(r):
+        pl.semaphore_wait(known.at[r], 2)
 
     switches = switch_ref[...]
     occ = switches[:16].astype(jnp.float32).astype(jnp.bfloat16)
@@ -148,7 +149,7 @@
             h[core, t, 0, :, cols] = r[:BLK]
             h[core, t, 1, :, cols] = r[BLK:]
         if t == 0:
-            pl.semaphore_wait(barrier, 24 - 4 * (z // 8))
+            pl.semaphore_wait(barrier, 11)
         for d in range(2):
             hop(d, t).start()
         for d in range(2):
@@ -185,8 +186,6 @@
             hop(d, slot).wait_recv()
             if slot < 4:
                 hop(d, slot + 2).start()
-            elif slot == 4:
-                hop(d, 6).start()
         for d in range(2):
             sender = (y + s) % Y if d == 0 else (y + Y - s) % Y
             parts = pair((t + sender // 4 + high) % 2, d, slot, d == 0)
@@ -195,6 +194,11 @@
                     blk[s - 1][who, d] = parts[who]
                 else:
                     blk[s - 1][who, d] += parts[who]
+
+    def last_hop():
+        for d in range(2):
+            hop(d, 5).wait_send()
+            hop(d, 6).start()
 
     def antipode():
         for d in range(2):
@@ -325,16 +329,23 @@
                         v = full[g][k, 0]
                         put((y + 4) % Y, k, v if side == 0 else v.T)
 
+    tell(0)
+    hear(0)
+    tell(1)
     ring_step(1, 0)
+    hear(1)
+    tell(2)
     ring_step(1, 1)
     xrs_start(0)
     ring_step(2, 0)
+    hear(2)
     zrs_start(0)
     ring_step(2, 1)
     xrs_start(1)
     ring_step(3, 0)
     ex_start(0)
     zrs_start(1)
+    last_hop()
     ring_step(3, 1)
     xrs_start(2)
     zag_start(0)
@@ -361,7 +372,7 @@
         for d in range(2):
             to_partner(t, d).wait_send()
     for d in range(2):
-        for slot in range(7):
+        for slot in (0, 1, 2, 3, 4, 6):
             hop(d, slot).wait_send()
     for g in range(GROUPS):
         wait_bytes(xa[g], xs_s.at[g])
@@ -413,6 +424,7 @@
             dma((2, 2)), dma((2, 2)),
             dma((2, 7)), dma((2, 7)),
             *[dma((GROUPS,))] * 12,
+            pltpu.SemaphoreType.REGULAR((3,)),
         ],
         compiler_params=pltpu.CompilerParams(
             collective_id=0, has_side_effects=True, vmem_limit_bytes=52 * 2**20),

time: 81.4 us -> 79.2 us (0.973)
  Pallas kernels: 79.5 us -> 77.3 us
    pallas_call x1, Pallas kernels: 79.5 us -> 77.3 us  [on_device(): pl.pallas_call(kernel, out_shape=jax.ShapeDtypeStruct((BLK, norb), f32),...]
where the time goes in v8:
time: 79.2 us; the launch traced here: 79 us
  Pallas kernels  77.3 us (98%)
  local copies, waits for them, and re-layouts  0.97 us (1%)
    pallas_call x1, Pallas kernels, on_device(): pl.pallas_call(kernel, out_shape=jax.ShapeDtypeStruct((BLK, norb), f32),...  77.3 us

profile of v8, /device:TPU:1, one launch (start us, length us, event | category | flops | bytes accessed | tf_op | source)
XLA Modules:
  0.0 79.0 jit_solution(18012717008974426178)
XLA Ops:
  0.0 0.7 pad_add_fusion.switch_ref
  0.7 77.3 %shard_map.46 = f32[128,2048]{1,0:T(8,128)S(1)} custom-call(bf16[4,128,2048]{2,1,0:T(8,128)(2,1)} %t_hbm.1, bf16[2048,768]{1,0:T(8,128)(2,1)} %c_hbm.1, s32[24,48]{1,0:T(8,128)S(1)} %pad_add_fusion.switch_ref), custom_call_target="tpu_custom_call" | custom-call | flops 3000000000 | bytes 6000000 | tf_op jit(solution)/shard_map/pallas_call | solution.py:405
  78.0 1.0 %copy.6 = f32[128,2048]{1,0:T(8,128)} copy(f32[128,2048]{1,0:T(8,128)S(1)} %shard_map.46) | data formatting | bytes 2097152

commit v9 on v8

--- a/solution.py
+++ b/solution.py
@@ -144,14 +144,19 @@
             tv[p] = tv[p] * own_mask
         lhs = tv[2 * t:2 * t + 2].reshape(2 * BLK, tv.shape[2])
         for n in range(nocc // 256):
-            cols = slice(n * 256, (n + 1) * 256)
+            cols = pl.ds(n * 256, 256)
             r = jnp.dot(lhs, cv[:, cols], preferred_element_type=jnp.float32).astype(jnp.bfloat16)
             h[core, t, 0, :, cols] = r[:BLK]
             h[core, t, 1, :, cols] = r[BLK:]
-        if t == 0:
-            pl.semaphore_wait(barrier, 11)
-        for d in range(2):
-            hop(d, t).start()
+            if t == 0:
+                if n == 0:
+                    pl.semaphore_wait(barrier, 11)
+                for d in range(2):
+                    remote(h.at[core, t, d, :, cols], ring.at[d, t, :, cols],
+                           ring_s.at[d, t], ring_r.at[d, t], nexts[d]).start()
+        if t == 1:
+            for d in range(2):
+                hop(d, t).start()
         for d in range(2):
             to_partner(t, d).start()
 

time: 79.2 us -> 79.2 us (level)
  no operation moved by 1% of the time
where the time goes in v9:
time: 79.2 us; the launch traced here: 79 us
  Pallas kernels  77.3 us (98%)
  local copies, waits for them, and re-layouts  0.97 us (1%)
    pallas_call x1, Pallas kernels, on_device(): pl.pallas_call(kernel, out_shape=jax.ShapeDtypeStruct((BLK, norb), f32),...  77.3 us

profile of v9, /device:TPU:1, one launch (start us, length us, event | category | flops | bytes accessed | tf_op | source)
XLA Modules:
  0.0 79.0 jit_solution(3788993166427852964)
XLA Ops:
  0.0 0.7 pad_add_fusion.switch_ref
  0.7 77.3 %shard_map.46 = f32[128,2048]{1,0:T(8,128)S(1)} custom-call(bf16[4,128,2048]{2,1,0:T(8,128)(2,1)} %t_hbm.1, bf16[2048,768]{1,0:T(8,128)(2,1)} %c_hbm.1, s32[24,48]{1,0:T(8,128)S(1)} %pad_add_fusion.switch_ref), custom_call_target="tpu_custom_call" | custom-call | flops 3000000000 | bytes 6000000 | tf_op jit(solution)/shard_map/pallas_call | solution.py:410
  78.0 1.0 %copy.6 = f32[128,2048]{1,0:T(8,128)} copy(f32[128,2048]{1,0:T(8,128)S(1)} %shard_map.46) | data formatting | bytes 2097152
